TPU v7x, 32 devices: a whole 2x2x4 slice. The times are simulated.
32 devices in a mesh: frag: 2 (over y), aux: 16 (over z, x, core).
Axes of the slice: x: 2, y: 2, z: 4, core: 2. Of those that a mesh axis runs over, the one named last changes fastest.
Arguments:
- blocks: bfloat16 [4096, 64, 128], P(('frag', 'aux')), parts along dimension 0, may hold values from -0.75 to 0.75
- slot_rows: int32 [4096], P(('frag', 'aux')), parts along dimension 0, may hold values from 0 to 15
- slot_shells: int32 [4096], P(('frag', 'aux')), parts along dimension 0, may hold values from 0 to 255, as said below
- shell_order: int32 [512], P('frag'), parts along dimension 0, may hold values from 0 to 255, as said below
- support: int32 [512, 2], P('frag'), parts along dimension 0, may hold values from 0 to 15
- coeffs: bfloat16 [512, 64, 128], P(('frag', 'aux')), parts along dimension 0, may hold values from -0.125 to 0.125
Outputs:
- exchange_matrix: float32 [2048, 1024], P(('frag', 'aux')), parts along dimension 0
There are 2 independent parts, one for each index of `frag`. A program takes and returns all parts, laid end to end along the dimension named above; each array names one. Nothing has to cross between parts.
Inputs may be any that keep to these rules, and one draw needn't show every extreme that they name: A permutation of the 256 shells; the device holding row k of coeffs holds the coefficients of shell shell_order[k]. `slot_shells`: of the 128 blocks of one aux block, at most 16 have column shells whose coefficients one device holds; in every draw some device holds the column shells of exactly 16 blocks of every aux block.
All inputs are finite; a program needn't handle non-finite values.
Results may differ from a plain program's by a relative error of at most 0.00098.
Values may be sent and summed in bfloat16 or wider, within the bound.
A program may use at most 64 MiB of HBM per device.

v0:
```python
import jax
import jax.numpy as jnp
from jax import lax
from jax.sharding import PartitionSpec as P

NOB = 16
ROWS = 16


def body(blocks, slot_rows, slot_shells, shell_order, support, coeffs):
    slot_count = blocks.shape[0]
    shell_size = blocks.shape[1]
    aux_width = blocks.shape[2]
    aux_local = aux_width // shell_size
    shell_total = shell_order.shape[0]
    supp_count = support.shape[1]
    orb_width = coeffs.shape[2] // supp_count
    match = shell_order[None, :] == slot_shells[:, None]
    position = jnp.sum(
        jnp.where(match, jnp.arange(shell_total, dtype=jnp.int32)[None, :], 0), axis=1
    )
    gathered = lax.all_gather(coeffs, "aux", axis=0, tiled=True)
    chosen_coef = gathered[position]
    half_blocks = jnp.einsum(
        "slo,slq->soq", chosen_coef, blocks, preferred_element_type=jnp.float32
    ).astype(jnp.bfloat16)
    orbital_ids = support[slot_shells]
    row_hot = slot_rows[:, None] == jnp.arange(ROWS, dtype=jnp.int32)[None, :]
    orbital_hot = orbital_ids[:, :, None] == jnp.arange(NOB, dtype=jnp.int32)[None, None, :]
    placement = (row_hot[:, None, :, None] & orbital_hot[:, :, None, :]).astype(jnp.bfloat16)
    placement = placement.reshape(slot_count * supp_count, ROWS * NOB)
    flat_half = half_blocks.reshape(slot_count * supp_count, orb_width * aux_width)
    summed = lax.dot_general(
        placement, flat_half, (((0,), (0,)), ((), ())), preferred_element_type=jnp.float32
    ).astype(jnp.bfloat16)
    summed = summed.reshape(ROWS, NOB, orb_width, aux_local, shell_size).transpose(0, 4, 1, 2, 3)
    stacked = summed.reshape(ROWS * shell_size, NOB * orb_width * aux_local)
    return lax.psum_scatter(
        lax.dot_general(
            stacked, stacked, (((1,), (1,)), ((), ())), preferred_element_type=jnp.float32
        ),
        "aux",
        scatter_dimension=0,
        tiled=True,
    )


def solution(mesh):
    return jax.shard_map(
        body,
        mesh=mesh,
        in_specs=(
            P(("frag", "aux"), None, None),
            P(("frag", "aux")),
            P(("frag", "aux")),
            P("frag"),
            P("frag", None),
            P(("frag", "aux"), None, None),
        ),
        out_specs=P(("frag", "aux"), None),
        check_vma=False,
    )
```

profile of v0, /device:TPU:1, one launch (start us, length us, event | category | flops | bytes accessed | tf_op | source)
XLA Modules:
  0.0 218.0 jit_solution(7987868896182448039)
XLA Ops:
  6.5 0.0 copy-start
  6.5 0.0 all-gather.2.cloned.1.call-start
  6.5 0.7 all-gather.2.cloned.1.call-update
  7.3 0.0 reduce-scatter.2.cloned.1.call-start
  7.3 0.8 copy.12
  8.1 0.7 compare_select_fusion.1
  8.8 0.6 gather_fusion
  9.4 0.7 iota_compare_fusion.1
  10.2 0.2 iota_compare_fusion
  10.4 0.5 broadcast_and_fusion
  10.9 0.8 and.26
  11.8 0.9 select_reduce_fusion
  12.7 49.9 %all-gather.2.cloned.1.call-done = bf16[256,64,128]{2,1,0:T(8,128)(2,1)} async-done(((bf16[16,64,128]{2,1,0:T(8,128)(2,1)}), bf16[256,64,128]{2,1,0:T(8,128)(2,1)}) %all-gather.2.cloned.1.call-update) | async-done | bytes 4194320 | tf_op jit(solution)/shard_map/all_gather | solution.py:22
  62.6 4.3 %gather_fusion.1 = bf16[128,64,128]{2,1,0:T(8,128)(2,1)} fusion(bf16[256,64,128]{2,1,0:T(8,128)(2,1)} %all-gather.2.cloned.1.call-done, s32[1024]{0:T(1024)S(1)} %pad_clamp_fusion), kind=kCustom, calls=%fused_computation.1 | custom fusion | bytes 4194816 | tf_op jit(solution)/shard_map/gather | solution.py:23
  66.9 0.0 copy-done
  66.9 4.9 %convolution_convert_fusion.1 = bf16[128,128,128]{2,1,0:T(8,128)(2,1)} fusion(bf16[128,64,128]{2,1,0:T(8,128)(2,1)} %gather_fusion.1, bf16[128,64,128]{2,1,0:T(8,128)(2,1)S(1)} %copy-done), kind=kOutput, calls=%fused_computation.4 | convolution fusion | flops 270532608 | bytes 8388608 | tf_op jit(solution)/shard_map/slo,slq->soq/dot_general | solution.py:24
  71.8 7.3 %reshape.61 = bf16[256,8192]{1,0:T(8,128)(2,1)} reshape(bf16[128,128,128]{2,1,0:T(8,128)(2,1)} %convolution_convert_fusion.1) | data formatting | bytes 8388608 | tf_op jit(solution)/shard_map/reshape | solution.py:32
  79.1 5.4 %convolution_convert_fusion = bf16[256,8192]{1,0:T(8,128)(2,1)} fusion(pred[256,256]{1,0:T(32,128)(4,1)S(1)} %and.26, bf16[256,8192]{1,0:T(8,128)(2,1)} %reshape.61), kind=kOutput, calls=%fused_computation.2 | convolution fusion | flops 1075838976 | bytes 8454144 | tf_op jit(solution)/shard_map/dot_general | solution.py:33
  84.6 15.6 %reshape.62 = bf16[16,16,64,2,64]{4,3,2,1,0:T(2,128)(2,1)} reshape(bf16[256,8192]{1,0:T(8,128)(2,1)} %convolution_convert_fusion) | data formatting | bytes 8388608 | tf_op jit(solution)/shard_map/reshape | solution.py:36
  100.1 20.1 %copy.15 = bf16[16,16,64,2,64]{4,0,3,2,1:T(8,128)(2,1)} copy(bf16[16,16,64,2,64]{4,3,2,1,0:T(2,128)(2,1)} %reshape.62) | data formatting | bytes 8388608 | tf_op jit(solution)/shard_map/reshape | solution.py:36
  120.2 11.9 %reshape.63 = bf16[1024,2048]{0,1:T(8,128)(2,1)} reshape(bf16[16,64,16,64,2]{1,0,4,3,2:T(8,128)(2,1)} %bitcast.19) | data formatting | bytes 8388608 | tf_op jit(solution)/shard_map/reshape | solution.py:37
  132.1 10.0 %fusion.1 = f32[1024,1024]{1,0:T(8,128)} fusion(bf16[1024,2048]{0,1:T(8,128)(2,1)} %reshape.63), kind=kOutput, calls=%fused_computation.14 | convolution fusion | flops 4294967296 | bytes 8388608 | tf_op jit(solution)/shard_map/dot_general | solution.py:39
  142.1 0.0 reduce-scatter.2.cloned.1.call-update
  142.1 69.1 %reduce-scatter.2.cloned.1.call-done = f32[64,1024]{1,0:T(8,128)} async-done(((f32[1024,1024]{1,0:T(8,128)}), f32[64,1024]{1,0:T(8,128)}) %reduce-scatter.2.cloned.1.call-update) | async-done | bytes 262160 | tf_op jit(solution)/shard_map/reduce_scatter | solution.py:38
  (3 shorter events, 0.0 us)
Async XLA Ops:
  6.5 60.4 %copy-start = (bf16[128,64,128]{2,1,0:T(8,128)(2,1)S(1)}, bf16[128,64,128]{2,1,0:T(8,128)(2,1)}, u32[]{:S(2)}) copy-start(bf16[128,64,128]{2,1,0:T(8,128)(2,1)} %param.6) | copy-start | bytes 6291460
  6.5 56.1 %all-gather.2.cloned.1.call-start = ((), (), s32[]{:S(2)}) async-start(), calls=%async_computation.1 | async-start | bytes 4456448 | tf_op jit(solution)/shard_map/all_gather | solution.py:22
  7.3 203.9 %reduce-scatter.2.cloned.1.call-start = ((), (), s32[]{:S(2)}) async-start(), calls=%async_computation.2 | async-start | bytes 4456448 | tf_op jit(solution)/shard_map/reduce_scatter | solution.py:38
Sparse Core Ops, SparseCore 0:
  9.5 53.0 all-gather.1
  142.2 68.9 reduce-scatter.1
where the time goes:
time: 221 us; the launch traced here: 218 us
  waiting for transfers between devices  120 us (54%)
  local copies, waits for them, and re-layouts  61.5 us (28%)
  matrix products  20.3 us (9%)
  between operations  13.5 us (6%)
  other arithmetic  3.01 us (1%)
    reduce_scatter x1, waiting for transfers between devices, body(): lax.psum_scatter(lax.dot_general(stacked, stacked, (((1,), (1,)), ((), ()...  69.1 us
    all_gather x1, waiting for transfers between devices, body(): gathered = lax.all_gather(coeffs, 'aux', axis=0, tiled=True)  49.9 us
    reshape x2, local copies, waits for them, and re-layouts, body(): summed.reshape(ROWS, NOB, orb_width, aux_local, shell_size)  35.7 us
    reshape x1, local copies, waits for them, and re-layouts, body(): stacked = summed.reshape(ROWS * shell_size, NOB * orb_width * aux_local)  11.9 us
    dot_general x1, matrix products, body(): lax.dot_general(stacked, stacked, (((1,), (1,)), ((), ())), preferred_ele...  9.99 us
    reshape x1, local copies, waits for them, and re-layouts, body(): half_blocks.reshape(slot_count * supp_count, orb_width * aux_width)  7.32 us
    dot_general x1, matrix products, body(): lax.dot_general(placement, flat_half, (((0,), (0,)), ((), ())), preferred...  5.44 us
    dot_general x1, matrix products, body(): jnp.einsum('slo,slq->soq', chosen_coef, blocks, preferred_element_type=jn...  4.86 us
  transfers between devices with their start and end apart: 2, of which 2 were waited for; matrix products, arithmetic and copies ran while one was open for 2% of the time, Pallas kernels for 0%

commit v1 on v0

v1 whole, which is shorter than its diff:
```python
import functools

import jax
import jax.numpy as jnp
from jax import lax
from jax.experimental import pallas as pl
from jax.experimental.pallas import tpu as pltpu
from jax.sharding import PartitionSpec as P

NOB = 16
ROWS = 16
NZ, NX, NC = 4, 2, 2
CHIPS = NZ * NX
REACH = CHIPS // 2


def device(z, x, c):
    return {"aux": (z * NX + x) * NC + c}


def here():
    me = lax.axis_index("aux")
    return me // (NX * NC), (me // NC) % NX, me % NC


def gather_kernel(own, out, local, z_recv, x_recv, m_recv, r_send, l_send, x_send, m_send):
    z, x, c = here()
    mate, across = device(z, x, 1 - c), device(z, 1 - x, c)

    keep = pltpu.make_async_copy(own, out.at[(z * NX + x) * NC + c], local)
    keep.start()
    barrier = pltpu.get_barrier_semaphore()
    pl.semaphore_signal(barrier, inc=1, device_id=mate)
    pl.semaphore_signal(barrier, inc=1, device_id=across)

    @pl.when(z > 0)
    def _():
        pl.semaphore_signal(barrier, inc=1, device_id=device(z - 1, x, c))

    @pl.when(z < NZ - 1)
    def _():
        pl.semaphore_signal(barrier, inc=1, device_id=device(z + 1, x, c))

    pl.semaphore_wait(barrier, 2 + jnp.where(z > 0, 1, 0) + jnp.where(z < NZ - 1, 1, 0))

    def copy(zz, xx, to, send, recv, first=False):
        spot = out.at[(zz * NX + xx) * NC + c]
        return pltpu.make_async_remote_copy(
            src_ref=own if first else spot, dst_ref=spot, send_sem=send, recv_sem=recv, device_id=to
        )

    def to_right(zz, first=False):
        return copy(zz, x, device(z + 1, x, c), r_send.at[zz], z_recv.at[zz], first)

    def to_left(zz, first=False):
        return copy(zz, x, device(z - 1, x, c), l_send.at[zz], z_recv.at[zz], first)

    def to_across(zz, first=False):
        return copy(zz, x, across, x_send.at[zz], x_recv.at[zz], first)

    def to_mate(zz, xx, first=False):
        spot = xx * NZ + zz
        return copy(zz, xx, mate, m_send.at[spot], m_recv.at[spot], first)

    def arrived_across(zz):
        pltpu.make_async_remote_copy(
            src_ref=own,
            dst_ref=out.at[(zz * NX + 1 - x) * NC + c],
            send_sem=x_send.at[zz],
            recv_sem=x_recv.at[zz],
            device_id=across,
        ).wait_recv()
        to_mate(zz, 1 - x).start()

    @pl.when(z < NZ - 1)
    def _():
        to_right(z, True).start()

    @pl.when(z > 0)
    def _():
        to_left(z, True).start()

    to_across(z, True).start()
    to_mate(z, x, True).start()
    for step in range(1, NZ):

        @pl.when(z - step >= 0)
        def _():
            zz = z - step
            copy(zz, x, across, r_send.at[zz], z_recv.at[zz]).wait_recv()

            @pl.when(z < NZ - 1)
            def _():
                to_right(zz).start()

            to_across(zz).start()
            to_mate(zz, x).start()

        @pl.when(z + step < NZ)
        def _():
            zz = z + step
            copy(zz, x, across, l_send.at[zz], z_recv.at[zz]).wait_recv()

            @pl.when(z > 0)
            def _():
                to_left(zz).start()

            to_across(zz).start()
            to_mate(zz, x).start()

        if step == 1:
            arrived_across(z)

    for step in range(1, NZ):

        @pl.when(z - step >= 0)
        def _():
            arrived_across(z - step)

        @pl.when(z + step < NZ)
        def _():
            arrived_across(z + step)

    keep.wait()
    for zz in range(NZ):

        @pl.when((zz <= z) & (z < NZ - 1))
        def _():
            to_right(zz).wait_send()

        @pl.when((zz >= z) & (z > 0))
        def _():
            to_left(zz).wait_send()

        to_across(zz).wait_send()
        for xx in range(NX):
            to_mate(zz, xx).wait_send()
            pltpu.make_async_remote_copy(
                src_ref=own,
                dst_ref=out.at[(zz * NX + xx) * NC + 1 - c],
                send_sem=m_send.at[xx * NZ + zz],
                recv_sem=m_recv.at[xx * NZ + zz],
                device_id=mate,
            ).wait_recv()


def gather_coeffs(coeffs):
    count = NZ * NX * NC
    dma = pltpu.SemaphoreType.DMA
    out = pl.pallas_call(
        gather_kernel,
        out_shape=jax.ShapeDtypeStruct((count,) + coeffs.shape, coeffs.dtype),
        in_specs=[pl.BlockSpec(memory_space=pl.ANY)],
        out_specs=pl.BlockSpec(memory_space=pl.ANY),
        scratch_shapes=[
            dma,
            dma((NZ,)),
            dma((NZ,)),
            dma((CHIPS,)),
            dma((NZ,)),
            dma((NZ,)),
            dma((NZ,)),
            dma((CHIPS,)),
        ],
        compiler_params=pltpu.CompilerParams(collective_id=0, has_side_effects=True),
        name="gather_coeffs",
    )(coeffs)
    return out.reshape((count * coeffs.shape[0],) + coeffs.shape[1:])


def fit_kernel(window, order, supp, rows, shells, coef, blocks, out, inv, acc, fit):
    shell_total = order.shape[0]
    slot_count, size, width = blocks.shape
    supp_count = supp.shape[0] // shell_total
    orb = coef.shape[2] // supp_count
    lanes = out.shape[1]
    tiles = ROWS * size // lanes
    depth = NOB * orb

    def invert(k, carry):
        inv[order[k]] = k
        return carry

    lax.fori_loop(0, shell_total, invert, 0, unroll=8)

    def clear(k, carry):
        acc[k] = jnp.zeros(acc.shape[1:], jnp.float32)
        return carry

    lax.fori_loop(0, ROWS * NOB, clear, 0, unroll=4)

    def slot(s, carry):
        shell = shells[s]
        row = rows[s]
        half = lax.dot_general(
            coef[inv[shell]], blocks[s], (((0,), (0,)), ((), ())), preferred_element_type=jnp.float32
        )
        half = half.astype(jnp.bfloat16).astype(jnp.float32)
        for a in range(supp_count):
            spot = row * NOB + supp[shell * supp_count + a]
            acc[spot] = acc[spot] + half[a * orb : (a + 1) * orb]
        return carry

    lax.fori_loop(0, slot_count, slot, 0, unroll=8)

    low = lax.broadcasted_iota(jnp.int32, (orb, width), 1) < size

    def regroup(b, carry):
        for j in range(tiles):
            even = acc[2 * j * NOB + b]
            odd = acc[(2 * j + 1) * NOB + b]
            first = jnp.where(low, even, pltpu.roll(odd, size, 1)).astype(jnp.bfloat16)
            second = jnp.where(low, pltpu.roll(even, size, 1), odd).astype(jnp.bfloat16)
            for col in range(j, fit.shape[1] // lanes, tiles):
                at = pl.ds(pl.multiple_of(b * orb, orb), orb)
                fit[at, col * lanes : (col + 1) * lanes] = first
                at = pl.ds(pl.multiple_of(depth + b * orb, orb), orb)
                fit[at, col * lanes : (col + 1) * lanes] = second
        return carry

    lax.fori_loop(0, NOB, regroup, 0)

    def multiply(i, carry):
        start = pl.multiple_of(i * lanes, lanes)
        right = fit[:, pl.ds(start, window)] if window < ROWS * size else fit[...]
        out[i] = lax.dot_general(
            fit[:, pl.ds(start, lanes)], right, (((0,), (0,)), ((), ())), preferred_element_type=jnp.float32
        )
        return carry

    lax.fori_loop(0, tiles, multiply, 0)


def fit_and_multiply(order, supp, rows, shells, coef, blocks, window):
    slot_count, size, width = blocks.shape
    orb = coef.shape[2] * order.shape[0] // supp.shape[0]
    full = ROWS * size
    held = full if window == full else full + window - width
    smem = pl.BlockSpec(memory_space=pltpu.SMEM)
    vmem = pl.BlockSpec(memory_space=pltpu.VMEM)
    return pl.pallas_call(
        functools.partial(fit_kernel, window),
        out_shape=jax.ShapeDtypeStruct((full // width, width, window), jnp.float32),
        in_specs=[smem] * 4 + [vmem] * 2,
        out_specs=vmem,
        scratch_shapes=[
            pltpu.SMEM(order.shape, jnp.int32),
            pltpu.VMEM((ROWS * NOB, orb, width), jnp.float32),
            pltpu.VMEM((NOB * orb * width // size, held), jnp.bfloat16),
        ],
        compiler_params=pltpu.CompilerParams(vmem_limit_bytes=48 * 2**20),
        name="fit_and_multiply",
    )(order, supp, rows, shells, coef, blocks)


def scatter_kernel(
    parts, out, mine, from_mate, from_across, from_line, mirror, total,
    local, m_send, m_recv, x_send, x_recv, z_send, z_recv, t_send, t_recv,
):
    z, x, c = here()
    chip = z * NX + x
    mate, across = device(z, x, 1 - c), device(z, 1 - x, c)

    def target(j):
        zz = (z + 1 + j % NZ) % NZ
        return zz * NX + (1 - x if j < NZ else x)

    keeps = []
    for j in range(CHIPS):
        keeps.append(pltpu.make_async_copy(parts.at[target(j) * NC + c], mine.at[j], local.at[j]))
        keeps[-1].start()

    barrier = pltpu.get_barrier_semaphore()
    me = lax.axis_index("aux")
    count = CHIPS * NC
    for step in range(1, count):
        pl.semaphore_signal(barrier, inc=1, device_id={"aux": lax.rem(me + step, count)})
    pl.semaphore_wait(barrier, count - 1)

    def send(src, dst, to, send_sem, recv_sem):
        copy = pltpu.make_async_remote_copy(
            src_ref=src, dst_ref=dst, send_sem=send_sem, recv_sem=recv_sem, device_id=to
        )
        copy.start()
        return copy

    to_mate = [
        send(parts.at[target(j) * NC + 1 - c], from_mate.at[j], mate, m_send.at[j], m_recv.at[j])
        for j in range(CHIPS)
    ]
    to_across = []
    for j in range(NZ):
        keeps[j].wait()
        to_mate[j].wait_recv()
        mine[j] = mine[j] + from_mate[j]
        to_across.append(send(mine.at[j], from_across.at[j], across, x_send.at[j], x_recv.at[j]))
    to_line = []
    for j in range(NZ):
        k = NZ + j
        keeps[k].wait()
        to_mate[k].wait_recv()
        mine[k] = mine[k] + from_mate[k]
    for j in range(NZ):
        k = NZ + j
        to_across[j].wait_recv()
        mine[k] = mine[k] + from_across[j]
        if j < NZ - 1:
            to_line.append(
                send(
                    mine.at[k],
                    from_line.at[j],
                    device(lax.rem(z + 1 + j, NZ), x, c),
                    z_send.at[j],
                    z_recv.at[j],
                )
            )
    for copy in to_line:
        copy.wait_recv()
    lanes = mirror.shape[3]
    for k in range(REACH + 1):
        cut = slice(k * lanes, (k + 1) * lanes)
        summed = mine[CHIPS - 1, :, cut]
        for j in range(NZ - 1):
            summed = summed + from_line[j, :, cut]
        total[k] = summed
    to_mirror = []
    for k in range(1, REACH):
        for e in range(NC):
            to_mirror.append(
                send(
                    total.at[k],
                    mirror.at[k - 1, c],
                    {"aux": lax.rem(chip + k, CHIPS) * NC + e},
                    t_send.at[k - 1, e],
                    t_recv.at[k - 1, c],
                )
            )
    for k in range(REACH + 1):
        at = pl.multiple_of(lax.rem(chip + k, CHIPS) * lanes, lanes)
        out[:, pl.ds(at, lanes)] = total[k]
    rows = out.shape[0]
    for k in range(1, REACH):
        for e in range(NC):
            pltpu.make_async_remote_copy(
                src_ref=total.at[k],
                dst_ref=mirror.at[k - 1, e],
                send_sem=t_send.at[k - 1, e],
                recv_sem=t_recv.at[k - 1, e],
                device_id=mate,
            ).wait_recv()
        turned = mirror[k - 1].reshape(NC * rows, lanes).T
        at = pl.multiple_of(lax.rem(chip + CHIPS - k, CHIPS) * lanes, lanes)
        out[:, pl.ds(at, lanes)] = jnp.where(c == 0, turned[:rows], turned[rows:])
    for copy in to_mate + to_across + to_line + to_mirror:
        copy.wait_send()


def scatter_sum(parts):
    tiles, lanes, window = parts.shape
    rows = lanes // NC
    parts = parts.reshape(tiles * NC, rows, window)
    dma = pltpu.SemaphoreType.DMA
    return pl.pallas_call(
        scatter_kernel,
        out_shape=jax.ShapeDtypeStruct((rows, tiles * lanes), jnp.float32),
        in_specs=[pl.BlockSpec(memory_space=pl.ANY)],
        out_specs=pl.BlockSpec(memory_space=pltpu.VMEM),
        scratch_shapes=[
            pltpu.VMEM((CHIPS, rows, window), jnp.float32),
            pltpu.VMEM((CHIPS, rows, window), jnp.float32),
            pltpu.VMEM((NZ, rows, window), jnp.float32),
            pltpu.VMEM((NZ - 1, rows, window), jnp.float32),
            pltpu.VMEM((REACH - 1, NC, rows, lanes), jnp.float32),
            pltpu.VMEM((REACH + 1, rows, lanes), jnp.float32),
            dma((CHIPS,)),
            dma((CHIPS,)),
            dma((CHIPS,)),
            dma((NZ,)),
            dma((NZ,)),
            dma((NZ - 1,)),
            dma((NZ - 1,)),
            dma((REACH - 1, NC)),
            dma((REACH - 1, NC)),
        ],
        compiler_params=pltpu.CompilerParams(
            collective_id=1, has_side_effects=True, vmem_limit_bytes=32 * 2**20
        ),
        name="scatter_sum",
    )(parts)


def body(near, blocks, slot_rows, slot_shells, shell_order, support, coeffs):
    full = ROWS * blocks.shape[1]
    supp = support.reshape(-1)
    if near:
        gathered = gather_coeffs(coeffs)
        window = (REACH + 1) * full // CHIPS
        parts = fit_and_multiply(shell_order, supp, slot_rows, slot_shells, gathered, blocks, window)
        return scatter_sum(parts)
    gathered = lax.all_gather(coeffs, "aux", axis=0, tiled=True)
    product = fit_and_multiply(shell_order, supp, slot_rows, slot_shells, gathered, blocks, full)
    return lax.psum_scatter(product.reshape(full, full), "aux", scatter_dimension=0, tiled=True)


def solution(mesh):
    return jax.shard_map(
        functools.partial(body, mesh.shape["aux"] == NZ * NX * NC),
        mesh=mesh,
        in_specs=(
            P(("frag", "aux"), None, None),
            P(("frag", "aux")),
            P(("frag", "aux")),
            P("frag"),
            P("frag", None),
            P(("frag", "aux"), None, None),
        ),
        out_specs=P(("frag", "aux"), None),
        check_vma=False,
    )
```

time: 221 us -> 82.9 us (0.38)
  waiting for transfers between devices: 120 us -> 0 us
  Pallas kernels: 0 us -> 80.2 us
  local copies, waits for them, and re-layouts: 61.5 us -> 1.82 us
  matrix products: 20.3 us -> 0 us
  between operations: 13.5 us -> 0.08 us
  other arithmetic: 3.01 us -> 0 us
    pallas_call x0 -> x3, Pallas kernels: none -> 80.2 us  [the longest x1 33.5 us: gather_coeffs(): pl.pallas_call(gather_kernel, out_shape=jax.ShapeDtypeStruct((count,) + c...]
    reduce_scatter x1 -> x0, waiting for transfers between devices: 69.1 us -> none  [body(): lax.psum_scatter(lax.dot_general(stacked, stacked, (((1,), (1,)), ((), ()...]
    reshape x4 -> x1, local copies, waits for them, and re-layouts: 54.9 us -> 0.14 us  [body(): supp = support.reshape(-1)]
    all_gather x1 -> x0, waiting for transfers between devices: 49.9 us -> none  [body(): gathered = lax.all_gather(coeffs, 'aux', axis=0, tiled=True)]
    dot_general x3 -> x0, matrix products: 20.3 us -> none  [the longest x1 9.99 us: body(): lax.dot_general(stacked, stacked, (((1,), (1,)), ((), ())), preferred_ele...]
    gather x2 -> x0, local copies, waits for them, and re-layouts: 4.96 us -> none  [the longest x1 4.32 us: body(): chosen_coef = gathered[position]]
  transfers between devices with their start and end apart: 2 -> 0, of which waited for: 2 -> 0; matrix products, arithmetic and copies ran while one was open for 2% -> 0% of each run, Pallas kernels for 0% -> 0%
where the time goes in v1:
time: 82.9 us; the launch traced here: 82.1 us
  Pallas kernels  80.2 us (97%)
  local copies, waits for them, and re-layouts  1.82 us (2%)
    pallas_call x1, Pallas kernels, gather_coeffs(): pl.pallas_call(gather_kernel, out_shape=jax.ShapeDtypeStruct((count,) + c...  33.5 us
    pallas_call x1, Pallas kernels, scatter_sum(): pl.pallas_call(scatter_kernel, out_shape=jax.ShapeDtypeStruct((rows, tile...  31.4 us
    pallas_call x1, Pallas kernels, fit_and_multiply(): pl.pallas_call(functools.partial(fit_kernel, window), out_shape=jax.Shape...  15.2 us
    unnamed x10, local copies, waits for them, and re-layouts  1.68 us

profile of v1, /device:TPU:1, one launch (start us, length us, event | category | flops | bytes accessed | tf_op | source)
XLA Modules:
  0.0 82.1 jit_solution(14909587310732378621)
XLA Ops:
  0.0 0.0 copy-start.1
  0.0 0.0 copy-start.3
  0.0 0.0 copy-start.2
  0.0 0.0 copy-start
  0.0 1.0 %copy.7 = s32[256,2]{1,0:T(8,128)S(1)} copy(s32[256,2]{0,1:T(2,128)} %param.10) | data formatting | bytes 4096 | tf_op args[4]
  1.0 0.1 reshape.9.supp
  1.1 33.5 %gather_coeffs.1 = bf16[16,16,64,128]{3,2,1,0:T(8,128)(2,1)} custom-call(bf16[16,64,128]{2,1,0:T(8,128)(2,1)} %own.1), custom_call_target="tpu_custom_call" | custom-call | tf_op jit(solution)/shard_map/gather_coeffs/pallas_call | solution.py:150
  34.7 0.0 copy-done.1
  34.7 0.0 copy-done.3
  34.7 0.0 copy-done.2
  34.7 0.0 copy-done
  34.7 15.2 %fit_and_multiply.1 = f32[8,128,640]{2,1,0:T(8,128)S(1)} custom-call(s32[256]{0:T(256)S(1)} %copy-done.1, s32[512]{0:T(512)S(1)} %reshape.9.supp, s32[128]{0:T(128)S(1)} %copy-done.2, s32[128]{0:T(128)S(1)} %copy-done.3, bf16[256,64,128]{2,1,0:T(8,128)(2,1)} %bitcast.3, bf16[128,64,128]{2,1,0:T(8,128)(2,1)S(1)} %copy-done), custom_call_target="tpu_custom_call" | custom-call | tf_op jit(solution)/shard_map/fit_and_multiply/pallas_call | solution.py:241
  49.9 31.4 %scatter_sum.1 = f32[64,1024]{1,0:T(8,128)S(1)} custom-call(f32[16,64,640]{2,1,0:T(8,128)S(1)} %bitcast.2), custom_call_target="tpu_custom_call" | custom-call | tf_op jit(solution)/shard_map/scatter_sum/pallas_call | solution.py:363
  81.4 0.7 copy.9
Async XLA Ops:
  0.0 34.7 %copy-start.1 = (s32[256]{0:T(256)S(1)}, s32[256]{0:T(256)}, u32[]{:S(2)}) copy-start(s32[256]{0:T(256)} %order.1) | copy-start | bytes 3076
  0.0 34.7 %copy-start.3 = (s32[128]{0:T(128)S(1)}, s32[128]{0:T(128)}, u32[]{:S(2)}) copy-start(s32[128]{0:T(128)} %shells.1) | copy-start | bytes 1540
  0.0 34.7 %copy-start.2 = (s32[128]{0:T(128)S(1)}, s32[128]{0:T(128)}, u32[]{:S(2)}) copy-start(s32[128]{0:T(128)} %rows.1) | copy-start | bytes 1540
  0.0 34.7 %copy-start = (bf16[128,64,128]{2,1,0:T(8,128)(2,1)S(1)}, bf16[128,64,128]{2,1,0:T(8,128)(2,1)}, u32[]{:S(2)}) copy-start(bf16[128,64,128]{2,1,0:T(8,128)(2,1)} %blocks.1) | copy-start | bytes 6291460

commit v2 on v1

--- a/solution.py
+++ b/solution.py
@@ -168,13 +168,12 @@
     return out.reshape((count * coeffs.shape[0],) + coeffs.shape[1:])
 
 
-def fit_kernel(window, order, supp, rows, shells, coef, blocks, out, inv, acc, fit):
+def fit_kernel(order, supp, rows, shells, coef, blocks, fit, inv, acc):
     shell_total = order.shape[0]
     slot_count, size, width = blocks.shape
-    supp_count = supp.shape[0] // shell_total
+    supp_count = supp.shape[0]
     orb = coef.shape[2] // supp_count
-    lanes = out.shape[1]
-    tiles = ROWS * size // lanes
+    tiles = fit.shape[1] // width
     depth = NOB * orb
 
     def invert(k, carry):
@@ -197,7 +196,7 @@
         )
         half = half.astype(jnp.bfloat16).astype(jnp.float32)
         for a in range(supp_count):
-            spot = row * NOB + supp[shell * supp_count + a]
+            spot = row * NOB + supp[a, shell]
             acc[spot] = acc[spot] + half[a * orb : (a + 1) * orb]
         return carry
 
@@ -211,70 +210,60 @@
             odd = acc[(2 * j + 1) * NOB + b]
             first = jnp.where(low, even, pltpu.roll(odd, size, 1)).astype(jnp.bfloat16)
             second = jnp.where(low, pltpu.roll(even, size, 1), odd).astype(jnp.bfloat16)
-            for col in range(j, fit.shape[1] // lanes, tiles):
-                at = pl.ds(pl.multiple_of(b * orb, orb), orb)
-                fit[at, col * lanes : (col + 1) * lanes] = first
-                at = pl.ds(pl.multiple_of(depth + b * orb, orb), orb)
-                fit[at, col * lanes : (col + 1) * lanes] = second
+            cut = slice(j * width, (j + 1) * width)
+            fit[pl.ds(pl.multiple_of(b * orb, orb), orb), cut] = first
+            fit[pl.ds(pl.multiple_of(depth + b * orb, orb), orb), cut] = second
         return carry
 
     lax.fori_loop(0, NOB, regroup, 0)
 
-    def multiply(i, carry):
-        start = pl.multiple_of(i * lanes, lanes)
-        right = fit[:, pl.ds(start, window)] if window < ROWS * size else fit[...]
-        out[i] = lax.dot_general(
-            fit[:, pl.ds(start, lanes)], right, (((0,), (0,)), ((), ())), preferred_element_type=jnp.float32
-        )
-        return carry
-
-    lax.fori_loop(0, tiles, multiply, 0)
-
-
-def fit_and_multiply(order, supp, rows, shells, coef, blocks, window):
-    slot_count, size, width = blocks.shape
-    orb = coef.shape[2] * order.shape[0] // supp.shape[0]
-    full = ROWS * size
-    held = full if window == full else full + window - width
+
+def fit_rows(order, supp, rows, shells, coef, blocks):
+    size, width = blocks.shape[1:]
+    orb = coef.shape[2] // supp.shape[0]
     smem = pl.BlockSpec(memory_space=pltpu.SMEM)
     vmem = pl.BlockSpec(memory_space=pltpu.VMEM)
     return pl.pallas_call(
-        functools.partial(fit_kernel, window),
-        out_shape=jax.ShapeDtypeStruct((full // width, width, window), jnp.float32),
+        fit_kernel,
+        out_shape=jax.ShapeDtypeStruct((NOB * orb * width // size, ROWS * size), jnp.bfloat16),
         in_specs=[smem] * 4 + [vmem] * 2,
         out_specs=vmem,
         scratch_shapes=[
             pltpu.SMEM(order.shape, jnp.int32),
             pltpu.VMEM((ROWS * NOB, orb, width), jnp.float32),
-            pltpu.VMEM((NOB * orb * width // size, held), jnp.bfloat16),
         ],
-        compiler_params=pltpu.CompilerParams(vmem_limit_bytes=48 * 2**20),
-        name="fit_and_multiply",
+        compiler_params=pltpu.CompilerParams(vmem_limit_bytes=40 * 2**20),
+        name="fit_rows",
     )(order, supp, rows, shells, coef, blocks)
 
 
 def scatter_kernel(
-    parts, out, mine, from_mate, from_across, from_line, mirror, total,
+    fit, out, held, part, mine, from_mate, from_across, from_line, mirror, total,
     local, m_send, m_recv, x_send, x_recv, z_send, z_recv, t_send, t_recv,
 ):
     z, x, c = here()
     chip = z * NX + x
     mate, across = device(z, x, 1 - c), device(z, 1 - x, c)
-
-    def target(j):
-        zz = (z + 1 + j % NZ) % NZ
-        return zz * NX + (1 - x if j < NZ else x)
-
-    keeps = []
-    for j in range(CHIPS):
-        keeps.append(pltpu.make_async_copy(parts.at[target(j) * NC + c], mine.at[j], local.at[j]))
-        keeps[-1].start()
+    full = fit.shape[1]
+    lanes = mirror.shape[3]
+    rows, window = mine.shape[1:]
+
+    keeps = [
+        pltpu.make_async_copy(fit, held.at[:, :full], local.at[0]),
+        pltpu.make_async_copy(
+            fit.at[:, : window - lanes], held.at[:, full : full + window - lanes], local.at[1]
+        ),
+    ]
+    for keep in keeps:
+        keep.start()
 
     barrier = pltpu.get_barrier_semaphore()
     me = lax.axis_index("aux")
     count = CHIPS * NC
     for step in range(1, count):
         pl.semaphore_signal(barrier, inc=1, device_id={"aux": lax.rem(me + step, count)})
+    for keep in keeps:
+        keep.wait()
     pl.semaphore_wait(barrier, count - 1)
 
     def send(src, dst, to, send_sem, recv_sem):
@@ -284,25 +273,55 @@
         copy.start()
         return copy
 
-    to_mate = [
-        send(parts.at[target(j) * NC + 1 - c], from_mate.at[j], mate, m_send.at[j], m_recv.at[j])
-        for j in range(CHIPS)
-    ]
-    to_across = []
-    for j in range(NZ):
-        keeps[j].wait()
-        to_mate[j].wait_recv()
-        mine[j] = mine[j] + from_mate[j]
-        to_across.append(send(mine.at[j], from_across.at[j], across, x_send.at[j], x_recv.at[j]))
+    own_rows = pl.ds(pl.multiple_of(c * rows, rows), rows)
+    mate_rows = pl.ds(pl.multiple_of((1 - c) * rows, rows), rows)
+
+    def to_mate(j):
+        return pltpu.make_async_remote_copy(
+            src_ref=part.at[j, mate_rows],
+            dst_ref=from_mate.at[j],
+            send_sem=m_send.at[j],
+            recv_sem=m_recv.at[j],
+            device_id=mate,
+        )
+
+    def to_across(j):
+        return pltpu.make_async_remote_copy(
+            src_ref=mine.at[j],
+            dst_ref=from_across.at[j],
+            send_sem=x_send.at[j],
+            recv_sem=x_recv.at[j],
+            device_id=across,
+        )
+
+    def packet(j, carry):
+        column = jnp.where(j < NZ, 1 - x, x)
+        start = pl.multiple_of((lax.rem(z + 1 + j, NZ) * NX + column) * lanes, lanes)
+        part[j] = lax.dot_general(
+            held[:, pl.ds(start, lanes)],
+            held[:, pl.ds(start, window)],
+            (((0,), (0,)), ((), ())),
+            preferred_element_type=jnp.float32,
+        )
+        to_mate(j).start()
+
+        @pl.when((j >= 1) & (j <= NZ))
+        def _():
+            to_mate(j - 1).wait_recv()
+            mine[j - 1] = part[j - 1, own_rows] + from_mate[j - 1]
+            to_across(j - 1).start()
+
+        return carry
+
+    lax.fori_loop(0, CHIPS, packet, 0)
     to_line = []
     for j in range(NZ):
         k = NZ + j
-        keeps[k].wait()
-        to_mate[k].wait_recv()
-        mine[k] = mine[k] + from_mate[k]
+        to_mate(k).wait_recv()
+        mine[k] = part[k, own_rows] + from_mate[k]
     for j in range(NZ):
         k = NZ + j
-        to_across[j].wait_recv()
+        to_across(j).wait_recv()
         mine[k] = mine[k] + from_across[j]
         if j < NZ - 1:
             to_line.append(
@@ -316,7 +335,6 @@
             )
     for copy in to_line:
         copy.wait_recv()
-    lanes = mirror.shape[3]
     for k in range(REACH + 1):
         cut = slice(k * lanes, (k + 1) * lanes)
         summed = mine[CHIPS - 1, :, cut]
@@ -338,7 +356,6 @@
     for k in range(REACH + 1):
         at = pl.multiple_of(lax.rem(chip + k, CHIPS) * lanes, lanes)
         out[:, pl.ds(at, lanes)] = total[k]
-    rows = out.shape[0]
     for k in range(1, REACH):
         for e in range(NC):
             pltpu.make_async_remote_copy(
@@ -351,28 +368,34 @@
         turned = mirror[k - 1].reshape(NC * rows, lanes).T
         at = pl.multiple_of(lax.rem(chip + CHIPS - k, CHIPS) * lanes, lanes)
         out[:, pl.ds(at, lanes)] = jnp.where(c == 0, turned[:rows], turned[rows:])
-    for copy in to_mate + to_across + to_line + to_mirror:
+    for j in range(CHIPS):
+        to_mate(j).wait_send()
+    for j in range(NZ):
+        to_across(j).wait_send()
+    for copy in to_line + to_mirror:
         copy.wait_send()
 
 
-def scatter_sum(parts):
-    tiles, lanes, window = parts.shape
-    rows = lanes // NC
-    parts = parts.reshape(tiles * NC, rows, window)
+def multiply_scatter(fit):
+    depth, full = fit.shape
+    lanes = full // CHIPS
+    rows, window = lanes // NC, (REACH + 1) * lanes
     dma = pltpu.SemaphoreType.DMA
     return pl.pallas_call(
         scatter_kernel,
-        out_shape=jax.ShapeDtypeStruct((rows, tiles * lanes), jnp.float32),
+        out_shape=jax.ShapeDtypeStruct((rows, full), jnp.float32),
         in_specs=[pl.BlockSpec(memory_space=pl.ANY)],
         out_specs=pl.BlockSpec(memory_space=pltpu.VMEM),
         scratch_shapes=[
+            pltpu.VMEM((depth, full + window - lanes), jnp.bfloat16),
+            pltpu.VMEM((CHIPS, lanes, window), jnp.float32),
             pltpu.VMEM((CHIPS, rows, window), jnp.float32),
             pltpu.VMEM((CHIPS, rows, window), jnp.float32),
             pltpu.VMEM((NZ, rows, window), jnp.float32),
             pltpu.VMEM((NZ - 1, rows, window), jnp.float32),
             pltpu.VMEM((REACH - 1, NC, rows, lanes), jnp.float32),
             pltpu.VMEM((REACH + 1, rows, lanes), jnp.float32),
-            dma((CHIPS,)),
+            dma((2,)),
             dma((CHIPS,)),
             dma((CHIPS,)),
             dma((NZ,)),
@@ -385,21 +408,17 @@
         compiler_params=pltpu.CompilerParams(
             collective_id=1, has_side_effects=True, vmem_limit_bytes=32 * 2**20
         ),
-        name="scatter_sum",
-    )(parts)
+        name="multiply_scatter",
+    )(fit)
 
 
 def body(near, blocks, slot_rows, slot_shells, shell_order, support, coeffs):
-    full = ROWS * blocks.shape[1]
-    supp = support.reshape(-1)
+    gathered = gather_coeffs(coeffs) if near else lax.all_gather(coeffs, "aux", axis=0, tiled=True)
+    fit = fit_rows(shell_order, support.T, slot_rows, slot_shells, gathered, blocks)
     if near:
-        gathered = gather_coeffs(coeffs)
-        window = (REACH + 1) * full // CHIPS
-        parts = fit_and_multiply(shell_order, supp, slot_rows, slot_shells, gathered, blocks, window)
-        return scatter_sum(parts)
-    gathered = lax.all_gather(coeffs, "aux", axis=0, tiled=True)
-    product = fit_and_multiply(shell_order, supp, slot_rows, slot_shells, gathered, blocks, full)
-    return lax.psum_scatter(product.reshape(full, full), "aux", scatter_dimension=0, tiled=True)
+        return multiply_scatter(fit)
+    product = lax.dot_general(fit, fit, (((0,), (0,)), ((), ())), preferred_element_type=jnp.float32)
+    return lax.psum_scatter(product, "aux", scatter_dimension=0, tiled=True)
 
 
 def solution(mesh):

time: 82.9 us -> 79.2 us (0.955)
  Pallas kernels: 80.2 us -> 76 us
  local copies, waits for them, and re-layouts: 1.82 us -> 2.91 us
    pallas_call x2, Pallas kernels: 46.6 us -> 42.5 us  [the longest x1 33.8 us: multiply_scatter(): pl.pallas_call(scatter_kernel, out_shape=jax.ShapeDtypeStruct((rows, full...]
    unnamed x10 -> x13, local copies, waits for them, and re-layouts: 1.68 us -> 2.91 us
where the time goes in v2:
time: 79.2 us; the launch traced here: 79 us
  Pallas kernels  76 us (96%)
  local copies, waits for them, and re-layouts  2.91 us (4%)
    pallas_call x1, Pallas kernels, multiply_scatter(): pl.pallas_call(scatter_kernel, out_shape=jax.ShapeDtypeStruct((rows, full...  33.8 us
    pallas_call x1, Pallas kernels, gather_coeffs(): pl.pallas_call(gather_kernel, out_shape=jax.ShapeDtypeStruct((count,) + c...  33.5 us
    pallas_call x1, Pallas kernels, fit_rows(): pl.pallas_call(fit_kernel, out_shape=jax.ShapeDtypeStruct((NOB * orb * wi...  8.73 us
    unnamed x13, local copies, waits for them, and re-layouts  2.91 us

profile of v2, /device:TPU:1, one launch (start us, length us, event | category | flops | bytes accessed | tf_op | source)
XLA Modules:
  0.0 79.0 jit_solution(4949831334228158734)
XLA Ops:
  0.0 0.0 copy-start.2
  0.0 0.0 copy-start.3
  0.0 0.0 copy-start.5
  0.0 0.0 copy-start.4
  0.0 0.0 copy-start.1
  0.0 33.5 %gather_coeffs.1 = bf16[16,16,64,128]{3,2,1,0:T(8,128)(2,1)} custom-call(bf16[16,64,128]{2,1,0:T(8,128)(2,1)} %own.1), custom_call_target="tpu_custom_call" | custom-call | tf_op jit(solution)/shard_map/gather_coeffs/pallas_call | solution.py:150
  33.6 0.0 copy-done.2
  33.6 0.0 copy-done.3
  33.6 0.0 copy-done.5
  33.6 0.0 copy-done.4
  33.6 0.0 copy-done.1
  33.6 0.0 copy-start
  33.6 2.2 %copy-done = bf16[16,16,64,128]{3,2,1,0:T(8,128)(2,1)S(1)} copy-done((bf16[16,16,64,128]{3,2,1,0:T(8,128)(2,1)S(1)}, bf16[16,16,64,128]{3,2,1,0:T(8,128)(2,1)}, u32[]{:S(2)}) %copy-start) | copy-done | bytes 4194328
  35.8 8.7 %fit_rows.1.fit = bf16[2048,1024]{1,0:T(8,128)(2,1)S(1)} custom-call(s32[256]{0:T(256)S(1)} %copy-done.3, s32[2,256]{1,0:T(2,128)S(1)} %bitcast.3, s32[128]{0:T(128)S(1)} %copy-done.4, s32[128]{0:T(128)S(1)} %copy-done.5, bf16[256,64,128]{2,1,0:T(8,128)(2,1)S(1)} %bitcast.2, bf16[128,64,128]{2,1,0:T(8,128)(2,1)S(1)} %copy-done.1), custom_call_target="tpu_custom_call" | custom-call | tf_op jit(solution)/shard_map/fit_rows/pallas_call | solution.py:226
  44.6 33.8 %multiply_scatter.1 = f32[64,1024]{1,0:T(8,128)S(1)} custom-call(bf16[2048,1024]{1,0:T(8,128)(2,1)S(1)} %fit_rows.1.fit), custom_call_target="tpu_custom_call" | custom-call | tf_op jit(solution)/shard_map/multiply_scatter/pallas_call | solution.py:384
  78.3 0.7 copy.8
Async XLA Ops:
  0.0 33.6 %copy-start.2 = (s32[256,2]{0,1:T(2,128)S(1)}, s32[256,2]{0,1:T(2,128)}, u32[]{:S(2)}) copy-start(s32[256,2]{0,1:T(2,128)} %param.10) | copy-start | bytes 6148
  0.0 33.6 %copy-start.3 = (s32[256]{0:T(256)S(1)}, s32[256]{0:T(256)}, u32[]{:S(2)}) copy-start(s32[256]{0:T(256)} %order.1) | copy-start | bytes 3076
  0.0 33.6 %copy-start.5 = (s32[128]{0:T(128)S(1)}, s32[128]{0:T(128)}, u32[]{:S(2)}) copy-start(s32[128]{0:T(128)} %shells.1) | copy-start | bytes 1540
  0.0 33.6 %copy-start.4 = (s32[128]{0:T(128)S(1)}, s32[128]{0:T(128)}, u32[]{:S(2)}) copy-start(s32[128]{0:T(128)} %rows.1) | copy-start | bytes 1540
  0.0 33.6 %copy-start.1 = (bf16[128,64,128]{2,1,0:T(8,128)(2,1)S(1)}, bf16[128,64,128]{2,1,0:T(8,128)(2,1)}, u32[]{:S(2)}) copy-start(bf16[128,64,128]{2,1,0:T(8,128)(2,1)} %blocks.1) | copy-start | bytes 6291460
  33.6 2.2 %copy-start = (bf16[16,16,64,128]{3,2,1,0:T(8,128)(2,1)S(1)}, bf16[16,16,64,128]{3,2,1,0:T(8,128)(2,1)}, u32[]{:S(2)}) copy-start(bf16[16,16,64,128]{3,2,1,0:T(8,128)(2,1)} %gather_coeffs.1) | copy-start | bytes 12582916

commit v3 on v2

--- a/solution.py
+++ b/solution.py
@@ -168,7 +168,9 @@
     return out.reshape((count * coeffs.shape[0],) + coeffs.shape[1:])
 
 
-def fit_kernel(order, supp, rows, shells, coef, blocks, fit, inv, acc):
+def fit_kernel(order, supp, rows, shells, gathered, blocks, fit, inv, acc, coef, loaded):
+    load = pltpu.make_async_copy(gathered, coef, loaded)
+    load.start()
     shell_total = order.shape[0]
     slot_count, size, width = blocks.shape
     supp_count = supp.shape[0]
@@ -187,6 +189,7 @@
         return carry
 
     lax.fori_loop(0, ROWS * NOB, clear, 0, unroll=4)
+    load.wait()
 
     def slot(s, carry):
         shell = shells[s]
@@ -226,19 +229,21 @@
     return pl.pallas_call(
         fit_kernel,
         out_shape=jax.ShapeDtypeStruct((NOB * orb * width // size, ROWS * size), jnp.bfloat16),
-        in_specs=[smem] * 4 + [vmem] * 2,
+        in_specs=[smem] * 4 + [pl.BlockSpec(memory_space=pl.ANY), vmem],
         out_specs=vmem,
         scratch_shapes=[
             pltpu.SMEM(order.shape, jnp.int32),
             pltpu.VMEM((ROWS * NOB, orb, width), jnp.float32),
+            pltpu.VMEM(coef.shape, coef.dtype),
+            pltpu.SemaphoreType.DMA,
         ],
-        compiler_params=pltpu.CompilerParams(vmem_limit_bytes=40 * 2**20),
+        compiler_params=pltpu.CompilerParams(vmem_limit_bytes=46 * 2**20),
         name="fit_rows",
     )(order, supp, rows, shells, coef, blocks)
 
 
 def scatter_kernel(
-    fit, out, held, part, mine, from_mate, from_across, from_line, mirror, total,
+    fit, out, held, part, from_mate, mine_a, mine_b, across_a, across_b, line_a, line_b, mirror, total,
     local, m_send, m_recv, x_send, x_recv, z_send, z_recv, t_send, t_recv,
 ):
     z, x, c = here()
@@ -246,7 +251,8 @@
     mate, across = device(z, x, 1 - c), device(z, 1 - x, c)
     full = fit.shape[1]
     lanes = mirror.shape[3]
-    rows, window = mine.shape[1:]
+    rows, window = from_mate.shape[1:]
+    mine, from_across, from_line = (mine_a, mine_b), (across_a, across_b), (line_a, line_b)
 
     keeps = [
         pltpu.make_async_copy(fit, held.at[:, :full], local.at[0]),
@@ -285,14 +291,21 @@
             device_id=mate,
         )
 
-    def to_across(j):
+    def to_across(g, j):
         return pltpu.make_async_remote_copy(
-            src_ref=mine.at[j],
-            dst_ref=from_across.at[j],
-            send_sem=x_send.at[j],
-            recv_sem=x_recv.at[j],
+            src_ref=mine[g].at[j],
+            dst_ref=from_across[g].at[j],
+            send_sem=x_send.at[g, j],
+            recv_sem=x_recv.at[g, j],
             device_id=across,
         )
+
+    def add_pair(j):
+        to_mate(j).wait_recv()
+        both = part[j, own_rows] + from_mate[j]
+        mine_a[j] = both[:, lanes : REACH * lanes]
+        mine_b[j, :, :lanes] = both[:, :lanes]
+        mine_b[j, :, lanes:] = both[:, REACH * lanes :]
 
     def packet(j, carry):
         column = jnp.where(j < NZ, 1 - x, x)
@@ -307,40 +320,47 @@
 
         @pl.when((j >= 1) & (j <= NZ))
         def _():
-            to_mate(j - 1).wait_recv()
-            mine[j - 1] = part[j - 1, own_rows] + from_mate[j - 1]
-            to_across(j - 1).start()
+            add_pair(j - 1)
+            to_across(0, j - 1).start()
 
         return carry
 
     lax.fori_loop(0, CHIPS, packet, 0)
     to_line = []
-    for j in range(NZ):
+
+    def pass_on(g, j):
         k = NZ + j
-        to_mate(k).wait_recv()
-        mine[k] = part[k, own_rows] + from_mate[k]
-    for j in range(NZ):
-        k = NZ + j
-        to_across(j).wait_recv()
-        mine[k] = mine[k] + from_across[j]
+        to_across(g, j).wait_recv()
+        mine[g][k] = mine[g][k] + from_across[g][j]
         if j < NZ - 1:
             to_line.append(
                 send(
-                    mine.at[k],
-                    from_line.at[j],
+                    mine[g].at[k],
+                    from_line[g].at[j],
                     device(lax.rem(z + 1 + j, NZ), x, c),
-                    z_send.at[j],
-                    z_recv.at[j],
+                    z_send.at[g, j],
+                    z_recv.at[g, j],
                 )
             )
-    for copy in to_line:
-        copy.wait_recv()
-    for k in range(REACH + 1):
-        cut = slice(k * lanes, (k + 1) * lanes)
-        summed = mine[CHIPS - 1, :, cut]
-        for j in range(NZ - 1):
-            summed = summed + from_line[j, :, cut]
-        total[k] = summed
+
+    def finish(g, blocks):
+        for copy in to_line[g * (NZ - 1) : (g + 1) * (NZ - 1)]:
+            copy.wait_recv()
+        for at, k in enumerate(blocks):
+            cut = slice(at * lanes, (at + 1) * lanes)
+            summed = mine[g][CHIPS - 1, :, cut]
+            for j in range(NZ - 1):
+                summed = summed + from_line[g][j, :, cut]
+            total[k] = summed
+
+    for j in range(NZ):
+        add_pair(NZ + j)
+    for j in range(NZ):
+        pass_on(0, j)
+        to_across(1, j).start()
+    pass_on(1, 0)
+    pass_on(1, 1)
+    finish(0, range(1, REACH))
     to_mirror = []
     for k in range(1, REACH):
         for e in range(NC):
@@ -353,6 +373,9 @@
                     t_recv.at[k - 1, c],
                 )
             )
+    for j in range(2, NZ):
+        pass_on(1, j)
+    finish(1, (0, REACH))
     for k in range(REACH + 1):
         at = pl.multiple_of(lax.rem(chip + k, CHIPS) * lanes, lanes)
         out[:, pl.ds(at, lanes)] = total[k]
@@ -370,8 +393,9 @@
         out[:, pl.ds(at, lanes)] = jnp.where(c == 0, turned[:rows], turned[rows:])
     for j in range(CHIPS):
         to_mate(j).wait_send()
-    for j in range(NZ):
-        to_across(j).wait_send()
+    for g in range(2):
+        for j in range(NZ):
+            to_across(g, j).wait_send()
     for copy in to_line + to_mirror:
         copy.wait_send()
 
@@ -380,6 +404,7 @@
     depth, full = fit.shape
     lanes = full // CHIPS
     rows, window = lanes // NC, (REACH + 1) * lanes
+    first = (REACH - 1) * lanes
     dma = pltpu.SemaphoreType.DMA
     return pl.pallas_call(
         scatter_kernel,
@@ -390,18 +415,21 @@
             pltpu.VMEM((depth, full + window - lanes), jnp.bfloat16),
             pltpu.VMEM((CHIPS, lanes, window), jnp.float32),
             pltpu.VMEM((CHIPS, rows, window), jnp.float32),
-            pltpu.VMEM((CHIPS, rows, window), jnp.float32),
-            pltpu.VMEM((NZ, rows, window), jnp.float32),
-            pltpu.VMEM((NZ - 1, rows, window), jnp.float32),
+            pltpu.VMEM((CHIPS, rows, first), jnp.float32),
+            pltpu.VMEM((CHIPS, rows, window - first), jnp.float32),
+            pltpu.VMEM((NZ, rows, first), jnp.float32),
+            pltpu.VMEM((NZ, rows, window - first), jnp.float32),
+            pltpu.VMEM((NZ - 1, rows, first), jnp.float32),
+            pltpu.VMEM((NZ - 1, rows, window - first), jnp.float32),
             pltpu.VMEM((REACH - 1, NC, rows, lanes), jnp.float32),
             pltpu.VMEM((REACH + 1, rows, lanes), jnp.float32),
             dma((2,)),
             dma((CHIPS,)),
             dma((CHIPS,)),
-            dma((NZ,)),
-            dma((NZ,)),
-            dma((NZ - 1,)),
-            dma((NZ - 1,)),
+            dma((2, NZ)),
+            dma((2, NZ)),
+            dma((2, NZ - 1)),
+            dma((2, NZ - 1)),
             dma((REACH - 1, NC)),
             dma((REACH - 1, NC)),
         ],

time: 79.2 us -> 76.9 us (0.971)
  local copies, waits for them, and re-layouts: 2.91 us -> 0.72 us
    unnamed x13 -> x11, local copies, waits for them, and re-layouts: 2.91 us -> 0.72 us
    pallas_call x1, Pallas kernels: 33.8 us -> 32.4 us  [multiply_scatter(): pl.pallas_call(scatter_kernel, out_shape=jax.ShapeDtypeStruct((rows, full...]
    pallas_call x1, Pallas kernels: 8.73 us -> 9.87 us  [fit_rows(): pl.pallas_call(fit_kernel, out_shape=jax.ShapeDtypeStruct((NOB * orb * wi...]
where the time goes in v3:
time: 76.9 us; the launch traced here: 76.6 us
  Pallas kernels  75.8 us (99%)
    pallas_call x1, Pallas kernels, gather_coeffs(): pl.pallas_call(gather_kernel, out_shape=jax.ShapeDtypeStruct((count,) + c...  33.5 us
    pallas_call x1, Pallas kernels, multiply_scatter(): pl.pallas_call(scatter_kernel, out_shape=jax.ShapeDtypeStruct((rows, full...  32.4 us
    pallas_call x1, Pallas kernels, fit_rows(): pl.pallas_call(fit_kernel, out_shape=jax.ShapeDtypeStruct((NOB * orb * wi...  9.87 us

profile of v3, /device:TPU:1, one launch (start us, length us, event | category | flops | bytes accessed | tf_op | source)
XLA Modules:
  0.0 76.6 jit_solution(4694944867914352319)
XLA Ops:
  0.0 0.0 copy-start.1
  0.0 0.0 copy-start.2
  0.0 0.0 copy-start.4
  0.0 0.0 copy-start.3
  0.0 0.0 copy-start
  0.0 33.5 %gather_coeffs.1 = bf16[16,16,64,128]{3,2,1,0:T(8,128)(2,1)} custom-call(bf16[16,64,128]{2,1,0:T(8,128)(2,1)} %own.1), custom_call_target="tpu_custom_call" | custom-call | tf_op jit(solution)/shard_map/gather_coeffs/pallas_call | solution.py:150
  33.6 0.0 copy-done.1
  33.6 0.0 copy-done.2
  33.6 0.0 copy-done.4
  33.6 0.0 copy-done.3
  33.6 0.0 copy-done
  33.6 9.9 %fit_rows.1.fit = bf16[2048,1024]{1,0:T(8,128)(2,1)S(1)} custom-call(s32[256]{0:T(256)S(1)} %copy-done.2, s32[2,256]{1,0:T(2,128)S(1)} %bitcast.2, s32[128]{0:T(128)S(1)} %copy-done.3, s32[128]{0:T(128)S(1)} %copy-done.4, bf16[256,64,128]{2,1,0:T(8,128)(2,1)} %bitcast.3, bf16[128,64,128]{2,1,0:T(8,128)(2,1)S(1)} %copy-done), custom_call_target="tpu_custom_call" | custom-call | tf_op jit(solution)/shard_map/fit_rows/pallas_call | solution.py:229
  43.5 32.4 %multiply_scatter.1 = f32[64,1024]{1,0:T(8,128)S(1)} custom-call(bf16[2048,1024]{1,0:T(8,128)(2,1)S(1)} %fit_rows.1.fit), custom_call_target="tpu_custom_call" | custom-call | tf_op jit(solution)/shard_map/multiply_scatter/pallas_call | solution.py:409
  75.9 0.7 copy.8
Async XLA Ops:
  0.0 33.6 %copy-start.1 = (s32[256,2]{0,1:T(2,128)S(1)}, s32[256,2]{0,1:T(2,128)}, u32[]{:S(2)}) copy-start(s32[256,2]{0,1:T(2,128)} %param.10) | copy-start | bytes 6148
  0.0 33.6 %copy-start.2 = (s32[256]{0:T(256)S(1)}, s32[256]{0:T(256)}, u32[]{:S(2)}) copy-start(s32[256]{0:T(256)} %order.1) | copy-start | bytes 3076
  0.0 33.6 %copy-start.4 = (s32[128]{0:T(128)S(1)}, s32[128]{0:T(128)}, u32[]{:S(2)}) copy-start(s32[128]{0:T(128)} %shells.1) | copy-start | bytes 1540
  0.0 33.6 %copy-start.3 = (s32[128]{0:T(128)S(1)}, s32[128]{0:T(128)}, u32[]{:S(2)}) copy-start(s32[128]{0:T(128)} %rows.1) | copy-start | bytes 1540
  0.0 33.6 %copy-start = (bf16[128,64,128]{2,1,0:T(8,128)(2,1)S(1)}, bf16[128,64,128]{2,1,0:T(8,128)(2,1)}, u32[]{:S(2)}) copy-start(bf16[128,64,128]{2,1,0:T(8,128)(2,1)} %blocks.1) | copy-start | bytes 6291460

commit v4 on v3

--- a/solution.py
+++ b/solution.py
@@ -191,19 +191,28 @@
     lax.fori_loop(0, ROWS * NOB, clear, 0, unroll=4)
     load.wait()
 
-    def slot(s, carry):
-        shell = shells[s]
-        row = rows[s]
-        half = lax.dot_general(
-            coef[inv[shell]], blocks[s], (((0,), (0,)), ((), ())), preferred_element_type=jnp.float32
-        )
-        half = half.astype(jnp.bfloat16).astype(jnp.float32)
-        for a in range(supp_count):
-            spot = row * NOB + supp[a, shell]
-            acc[spot] = acc[spot] + half[a * orb : (a + 1) * orb]
+    batch = 8 if slot_count % 8 == 0 else 1
+
+    def slots(n, carry):
+        halves = []
+        for s in range(batch):
+            shell = shells[n * batch + s]
+            half = lax.dot_general(
+                coef[inv[shell]],
+                blocks[n * batch + s],
+                (((0,), (0,)), ((), ())),
+                preferred_element_type=jnp.float32,
+            )
+            halves.append(half.astype(jnp.bfloat16).astype(jnp.float32))
+        for s, half in enumerate(halves):
+            shell = shells[n * batch + s]
+            row = rows[n * batch + s]
+            for a in range(supp_count):
+                spot = row * NOB + supp[a, shell]
+                acc[spot] = acc[spot] + half[a * orb : (a + 1) * orb]
         return carry
 
-    lax.fori_loop(0, slot_count, slot, 0, unroll=8)
+    lax.fori_loop(0, slot_count // batch, slots, 0, unroll=2)
 
     low = lax.broadcasted_iota(jnp.int32, (orb, width), 1) < size
 

time: 76.9 us -> 75.4 us (0.980)
  Pallas kernels: 75.8 us -> 74.3 us
    pallas_call x1, Pallas kernels: 9.87 us -> 8.34 us  [fit_rows(): pl.pallas_call(fit_kernel, out_shape=jax.ShapeDtypeStruct((NOB * orb * wi...]
where the time goes in v4:
time: 75.4 us; the launch traced here: 75.1 us
  Pallas kernels  74.3 us (99%)
    pallas_call x1, Pallas kernels, gather_coeffs(): pl.pallas_call(gather_kernel, out_shape=jax.ShapeDtypeStruct((count,) + c...  33.5 us
    pallas_call x1, Pallas kernels, multiply_scatter(): pl.pallas_call(scatter_kernel, out_shape=jax.ShapeDtypeStruct((rows, full...  32.4 us
    pallas_call x1, Pallas kernels, fit_rows(): pl.pallas_call(fit_kernel, out_shape=jax.ShapeDtypeStruct((NOB * orb * wi...  8.34 us

profile of v4, /device:TPU:1, one launch (start us, length us, event | category | flops | bytes accessed | tf_op | source)
XLA Modules:
  0.0 75.1 jit_solution(17624841494989116038)
XLA Ops:
  0.0 0.0 copy-start.1
  0.0 0.0 copy-start.2
  0.0 0.0 copy-start.4
  0.0 0.0 copy-start.3
  0.0 0.0 copy-start
  0.0 33.5 %gather_coeffs.1 = bf16[16,16,64,128]{3,2,1,0:T(8,128)(2,1)} custom-call(bf16[16,64,128]{2,1,0:T(8,128)(2,1)} %own.1), custom_call_target="tpu_custom_call" | custom-call | tf_op jit(solution)/shard_map/gather_coeffs/pallas_call | solution.py:150
  33.6 0.0 copy-done.1
  33.6 0.0 copy-done.2
  33.6 0.0 copy-done.4
  33.6 0.0 copy-done.3
  33.6 0.0 copy-done
  33.6 8.3 %fit_rows.1.fit = bf16[2048,1024]{1,0:T(8,128)(2,1)S(1)} custom-call(s32[256]{0:T(256)S(1)} %copy-done.2, s32[2,256]{1,0:T(2,128)S(1)} %bitcast.2, s32[128]{0:T(128)S(1)} %copy-done.3, s32[128]{0:T(128)S(1)} %copy-done.4, bf16[256,64,128]{2,1,0:T(8,128)(2,1)} %bitcast.3, bf16[128,64,128]{2,1,0:T(8,128)(2,1)S(1)} %copy-done), custom_call_target="tpu_custom_call" | custom-call | tf_op jit(solution)/shard_map/fit_rows/pallas_call | solution.py:238
  42.0 32.4 %multiply_scatter.1 = f32[64,1024]{1,0:T(8,128)S(1)} custom-call(bf16[2048,1024]{1,0:T(8,128)(2,1)S(1)} %fit_rows.1.fit), custom_call_target="tpu_custom_call" | custom-call | tf_op jit(solution)/shard_map/multiply_scatter/pallas_call | solution.py:418
  74.4 0.7 copy.8
Async XLA Ops:
  0.0 33.6 %copy-start.1 = (s32[256,2]{0,1:T(2,128)S(1)}, s32[256,2]{0,1:T(2,128)}, u32[]{:S(2)}) copy-start(s32[256,2]{0,1:T(2,128)} %param.10) | copy-start | bytes 6148
  0.0 33.6 %copy-start.2 = (s32[256]{0:T(256)S(1)}, s32[256]{0:T(256)}, u32[]{:S(2)}) copy-start(s32[256]{0:T(256)} %order.1) | copy-start | bytes 3076
  0.0 33.6 %copy-start.4 = (s32[128]{0:T(128)S(1)}, s32[128]{0:T(128)}, u32[]{:S(2)}) copy-start(s32[128]{0:T(128)} %shells.1) | copy-start | bytes 1540
  0.0 33.6 %copy-start.3 = (s32[128]{0:T(128)S(1)}, s32[128]{0:T(128)}, u32[]{:S(2)}) copy-start(s32[128]{0:T(128)} %rows.1) | copy-start | bytes 1540
  0.0 33.6 %copy-start = (bf16[128,64,128]{2,1,0:T(8,128)(2,1)S(1)}, bf16[128,64,128]{2,1,0:T(8,128)(2,1)}, u32[]{:S(2)}) copy-start(bf16[128,64,128]{2,1,0:T(8,128)(2,1)} %blocks.1) | copy-start | bytes 6291460

commit v5 on v4

--- a/solution.py
+++ b/solution.py
@@ -23,11 +23,18 @@
     return me // (NX * NC), (me // NC) % NX, me % NC
 
 
-def gather_kernel(own, out, local, z_recv, x_recv, m_recv, r_send, l_send, x_send, m_send):
+def gather_kernel(
+    whole, full_out, local, z_recv, x_recv, m_recv, r_send, l_send, x_send, m_send,
+    bz_recv, bx_recv, bm_recv, br_send, bl_send, bx_send, bm_send,
+):
+    held = whole.shape[0]
+    cut = held - held // 8
+    own, out = whole.at[:cut], full_out.at[:, :cut]
+    b_own, b_out = whole.at[cut:], full_out.at[:, cut:]
     z, x, c = here()
     mate, across = device(z, x, 1 - c), device(z, 1 - x, c)
 
-    keep = pltpu.make_async_copy(own, out.at[(z * NX + x) * NC + c], local)
+    keep = pltpu.make_async_copy(whole, full_out.at[(z * NX + x) * NC + c], local)
     keep.start()
     barrier = pltpu.get_barrier_semaphore()
     pl.semaphore_signal(barrier, inc=1, device_id=mate)
@@ -72,6 +79,36 @@
         ).wait_recv()
         to_mate(zz, 1 - x).start()
 
+    def b_copy(zz, xx, to, send, recv, first=False):
+        spot = b_out.at[(zz * NX + xx) * NC + c]
+        return pltpu.make_async_remote_copy(
+            src_ref=b_own if first else spot, dst_ref=spot, send_sem=send, recv_sem=recv, device_id=to
+        )
+
+    def b_right(zz, xx, first=False):
+        return b_copy(zz, xx, device(z + 1, x, c), br_send.at[zz, xx], bz_recv.at[zz, xx], first)
+
+    def b_left(zz, xx, first=False):
+        return b_copy(zz, xx, device(z - 1, x, c), bl_send.at[zz, xx], bz_recv.at[zz, xx], first)
+
+    def b_mate(zz, xx, first=False):
+        return b_copy(zz, xx, mate, bm_send.at[zz, xx], bm_recv.at[zz, xx], first)
+
+    def b_spread(xx, first):
+        @pl.when(z < NZ - 1)
+        def _():
+            b_right(z, xx, first).start()
+
+        @pl.when(z > 0)
+        def _():
+            b_left(z, xx, first).start()
+
+        b_mate(z, xx, first).start()
+
+    b_across = b_copy(z, x, across, bx_send, bx_recv, True)
+    b_across.start()
+    b_spread(x, True)
+
     @pl.when(z < NZ - 1)
     def _():
         to_right(z, True).start()
@@ -82,11 +119,21 @@
 
     to_across(z, True).start()
     to_mate(z, x, True).start()
+    b_copy(z, 1 - x, across, bx_send, bx_recv).wait_recv()
+    b_spread(1 - x, False)
     for step in range(1, NZ):
 
         @pl.when(z - step >= 0)
         def _():
             zz = z - step
+            for xx in range(NX):
+                b_copy(zz, xx, across, br_send.at[zz, xx], bz_recv.at[zz, xx]).wait_recv()
+
+                @pl.when(z < NZ - 1)
+                def _():
+                    b_right(zz, xx).start()
+
+                b_mate(zz, xx).start()
             copy(zz, x, across, r_send.at[zz], z_recv.at[zz]).wait_recv()
 
             @pl.when(z < NZ - 1)
@@ -99,6 +146,14 @@
         @pl.when(z + step < NZ)
         def _():
             zz = z + step
+            for xx in range(NX):
+                b_copy(zz, xx, across, bl_send.at[zz, xx], bz_recv.at[zz, xx]).wait_recv()
+
+                @pl.when(z > 0)
+                def _():
+                    b_left(zz, xx).start()
+
+                b_mate(zz, xx).start()
             copy(zz, x, across, l_send.at[zz], z_recv.at[zz]).wait_recv()
 
             @pl.when(z > 0)
@@ -122,7 +177,26 @@
             arrived_across(z + step)
 
     keep.wait()
+    b_across.wait_send()
     for zz in range(NZ):
+        for xx in range(NX):
+
+            @pl.when((zz <= z) & (z < NZ - 1))
+            def _():
+                b_right(zz, xx).wait_send()
+
+            @pl.when((zz >= z) & (z > 0))
+            def _():
+                b_left(zz, xx).wait_send()
+
+            b_mate(zz, xx).wait_send()
+            pltpu.make_async_remote_copy(
+                src_ref=b_own,
+                dst_ref=b_out.at[(zz * NX + xx) * NC + 1 - c],
+                send_sem=bm_send.at[zz, xx],
+                recv_sem=bm_recv.at[zz, xx],
+                device_id=mate,
+            ).wait_recv()
 
         @pl.when((zz <= z) & (z < NZ - 1))
         def _():
@@ -161,6 +235,13 @@
             dma((NZ,)),
             dma((NZ,)),
             dma((CHIPS,)),
+            dma((NZ, NX)),
+            dma,
+            dma((NZ, NX)),
+            dma((NZ, NX)),
+            dma((NZ, NX)),
+            dma,
+            dma((NZ, NX)),
         ],
         compiler_params=pltpu.CompilerParams(collective_id=0, has_side_effects=True),
         name="gather_coeffs",

time: 75.4 us -> 75.8 us (level)
  no operation moved by 1% of the time
where the time goes in v5:
time: 75.8 us; the launch traced here: 75.4 us
  Pallas kernels  74.6 us (98%)
    pallas_call x1, Pallas kernels, gather_coeffs(): pl.pallas_call(gather_kernel, out_shape=jax.ShapeDtypeStruct((count,) + c...  34 us
    pallas_call x1, Pallas kernels, multiply_scatter(): pl.pallas_call(scatter_kernel, out_shape=jax.ShapeDtypeStruct((rows, full...  32.3 us
    pallas_call x1, Pallas kernels, fit_rows(): pl.pallas_call(fit_kernel, out_shape=jax.ShapeDtypeStruct((NOB * orb * wi...  8.35 us

profile of v5, /device:TPU:1, one launch (start us, length us, event | category | flops | bytes accessed | tf_op | source)
XLA Modules:
  0.0 75.4 jit_solution(12117154408446047408)
XLA Ops:
  0.0 0.0 copy-start.1
  0.0 0.0 copy-start.2
  0.0 0.0 copy-start.4
  0.0 0.0 copy-start.3
  0.0 0.0 copy-start
  0.0 34.0 %gather_coeffs.1 = bf16[16,16,64,128]{3,2,1,0:T(8,128)(2,1)} custom-call(bf16[16,64,128]{2,1,0:T(8,128)(2,1)} %whole.1), custom_call_target="tpu_custom_call" | custom-call | tf_op jit(solution)/shard_map/gather_coeffs/pallas_call | solution.py:224
  34.0 0.0 copy-done.1
  34.0 0.0 copy-done.2
  34.1 0.0 copy-done.4
  34.1 0.0 copy-done.3
  34.1 0.0 copy-done
  34.1 8.4 %fit_rows.1.fit = bf16[2048,1024]{1,0:T(8,128)(2,1)S(1)} custom-call(s32[256]{0:T(256)S(1)} %copy-done.2, s32[2,256]{1,0:T(2,128)S(1)} %bitcast.2, s32[128]{0:T(128)S(1)} %copy-done.3, s32[128]{0:T(128)S(1)} %copy-done.4, bf16[256,64,128]{2,1,0:T(8,128)(2,1)} %bitcast.3, bf16[128,64,128]{2,1,0:T(8,128)(2,1)S(1)} %copy-done), custom_call_target="tpu_custom_call" | custom-call | tf_op jit(solution)/shard_map/fit_rows/pallas_call | solution.py:319
  42.4 32.3 %multiply_scatter.1 = f32[64,1024]{1,0:T(8,128)S(1)} custom-call(bf16[2048,1024]{1,0:T(8,128)(2,1)S(1)} %fit_rows.1.fit), custom_call_target="tpu_custom_call" | custom-call | tf_op jit(solution)/shard_map/multiply_scatter/pallas_call | solution.py:499
  74.7 0.7 copy.8
Async XLA Ops:
  0.0 34.0 %copy-start.1 = (s32[256,2]{0,1:T(2,128)S(1)}, s32[256,2]{0,1:T(2,128)}, u32[]{:S(2)}) copy-start(s32[256,2]{0,1:T(2,128)} %param.10) | copy-start | bytes 6148
  0.0 34.0 %copy-start.2 = (s32[256]{0:T(256)S(1)}, s32[256]{0:T(256)}, u32[]{:S(2)}) copy-start(s32[256]{0:T(256)} %order.1) | copy-start | bytes 3076
  0.0 34.1 %copy-start.4 = (s32[128]{0:T(128)S(1)}, s32[128]{0:T(128)}, u32[]{:S(2)}) copy-start(s32[128]{0:T(128)} %shells.1) | copy-start | bytes 1540
  0.0 34.1 %copy-start.3 = (s32[128]{0:T(128)S(1)}, s32[128]{0:T(128)}, u32[]{:S(2)}) copy-start(s32[128]{0:T(128)} %rows.1) | copy-start | bytes 1540
  0.0 34.1 %copy-start = (bf16[128,64,128]{2,1,0:T(8,128)(2,1)S(1)}, bf16[128,64,128]{2,1,0:T(8,128)(2,1)}, u32[]{:S(2)}) copy-start(bf16[128,64,128]{2,1,0:T(8,128)(2,1)} %blocks.1) | copy-start | bytes 6291460
